TPU v7x, 512 devices: a whole 4x4x16 slice. The times are simulated.
512 devices in a mesh: gz: 32 (over z_lo, x, core), gy: 16 (over z_hi, y).
Axes of the slice: x: 4, y: 4, z: 16 (z_hi: 4, z_lo: 4; z = z_hi * 4 + z_lo), core: 2. Of those that a mesh axis runs over, the one named last changes fastest.
Arguments:
- current: float32 [2, 256, 512, 512], P(None, 'gz', 'gy'), may hold values from -6 to 6
- kernel: float32 [2, 256, 512, 512], P(None, 'gz', 'gy'), may hold values from -6 to 6
Outputs:
- potential: float32 [2, 256, 512, 512], P(None, 'gz', 'gy')
All inputs are finite; a program needn't handle non-finite values.
Results may differ from a plain program's by a relative error of at most 0.00007.
Values sent between devices are 32-bit elements; how exact they have to be, the bound alone decides.
A program may use at most 64 MiB of HBM per device.

v0:
```python
import functools

import jax
import jax.numpy as jnp
import ml_dtypes
import numpy as np
from jax import lax
from jax.experimental import pallas as pl
from jax.experimental.pallas import tpu as pltpu
from jax.sharding import PartitionSpec as P

MESH = pl.DeviceIdType.MESH
F32 = jnp.float32
BF16 = jnp.bfloat16


def two_terms(table):
    high = table.astype(ml_dtypes.bfloat16)
    low = (table - high.astype(np.float64)).astype(ml_dtypes.bfloat16)
    return np.stack([high, low])


def dft_tables(length, groups):
    index = np.arange(length)
    angle = (index[:, None] * index[None, :] % length) * (2.0 * np.pi / length)
    cos, sin = np.cos(angle), np.sin(angle)
    full = np.block([[cos, sin], [-sin, cos]])
    block = length // groups
    rows = full.reshape(2, groups, block, 2 * length).transpose(1, 0, 2, 3)
    rows = rows.reshape(2 * length, 2 * length)
    return two_terms(rows), two_terms(full.T)


def split(value):
    high = value.astype(BF16)
    return high, (value - high.astype(F32)).astype(BF16)


def dot_nt(a, b):
    return lax.dot_general(a, b, (((1,), (1,)), ((), ())), preferred_element_type=F32)


def dot_nn(a, b):
    return jnp.dot(a, b, preferred_element_type=F32)


def regroup(pieces):
    lane = lax.broadcasted_iota(jnp.int32, pieces[0].shape, 1)
    low = lane < 64
    even = lax.rem(lane // 32, 2) == 0
    v0, v1, v2, v3 = pieces

    def halves(a, b):
        return (
            jnp.where(low, a, pltpu.roll(b, 64, 1)),
            jnp.where(low, pltpu.roll(a, 64, 1), b),
        )

    def quarters(a, b):
        return (
            jnp.where(even, a, pltpu.roll(b, 32, 1)),
            jnp.where(even, pltpu.roll(a, 96, 1), b),
        )

    a0, a2 = halves(v0, v2)
    a1, a3 = halves(v1, v3)
    return quarters(a0, a1) + quarters(a2, a3)


def body(
    members,
    groups,
    scale,
    cur,
    kern,
    nt_hbm,
    nn_hbm,
    out,
    nt,
    nn,
    rhs,
    lhs1,
    lhs2,
    kmir,
    t1,
    r1,
    t2,
    r2,
    table_sem,
    k_send,
    k_recv,
    send1,
    recv1,
    send2,
    recv2,
):
    gz = lax.axis_index("gz")
    gy = lax.axis_index("gy")
    mirror = members - 1 - gz
    zh = gy // 4
    yc = lax.rem(gy, 4)

    load_nt = pltpu.make_async_copy(nt_hbm, nt, table_sem.at[0])
    load_nn = pltpu.make_async_copy(nn_hbm, nn, table_sem.at[1])
    load_nt.start()
    load_nn.start()

    def peer(side, dz, dy):
        other = lax.rem(zh + dz, 4) * 4 + lax.rem(yc + dy, 4)
        return gz + side * (mirror - gz), other

    barrier = pltpu.get_barrier_semaphore()

    def greet(e, carry):
        where = peer(e // 16, lax.rem(e // 4, 4), lax.rem(e, 4))
        pl.semaphore_signal(barrier, inc=1, device_id=where, device_id_type=MESH)
        return carry

    lax.fori_loop(1, 32, greet, 0)
    pl.semaphore_wait(barrier, 31)

    def kernel_copy(part):
        return pltpu.make_async_remote_copy(
            src_ref=kern.at[part, pl.ds(4, 4)],
            dst_ref=kmir.at[part],
            send_sem=k_send.at[part],
            recv_sem=k_recv.at[part],
            device_id=(mirror, gy),
            device_id_type=MESH,
        )

    kernel_copy(0).start()
    kernel_copy(1).start()

    def block_copy(t, r, send, recv, e):
        side = e // 16
        g, other = peer(side, lax.rem(e // 4, 4), lax.rem(e, 4))
        return pltpu.make_async_remote_copy(
            src_ref=t.at[side, other],
            dst_ref=r.at[side, gy],
            send_sem=send.at[e],
            recv_sem=recv.at[e],
            device_id=(g, other),
            device_id_type=MESH,
        )

    def transform_and_send(t, r, send, recv):
        def step(i, carry):
            dz = lax.rem(i + 1, 4)
            zb = lax.rem(zh + dz, 4)
            rows = pl.ds(pl.multiple_of(zb * 256, 256), 256)
            high, low = nt[0, rows, :], nt[1, rows, :]
            total = dot_nt(high, rhs[0]) + dot_nt(high, rhs[1]) + dot_nt(low, rhs[0])
            t[0, pl.ds(zb * 4, 4)] = total[:, :128].reshape(4, 64, 128)
            t[1, pl.ds(zb * 4, 4)] = total[:, 128:].reshape(4, 64, 128)

            def send_one(q, inner):
                e = (q // 4) * 16 + dz * 4 + lax.rem(q, 4)

                @pl.when(e > 0)
                def _():
                    block_copy(t, r, send, recv, e).start()

                return inner

            return lax.fori_loop(0, 8, send_one, carry)

        lax.fori_loop(0, 4, step, 0)
        r[0, gy] = t[0, gy]

    def receive_all(t, r, send, recv):
        def one(e, carry):
            block_copy(t, r, send, recv, e).wait_recv()
            return carry

        lax.fori_loop(1, 32, one, 0)

    def sent_all(t, r, send, recv):
        def one(e, carry):
            block_copy(t, r, send, recv, e).wait_send()
            return carry

        lax.fori_loop(1, 32, one, 0)

    for part in range(2):
        for place in range(8):
            plane = place if place < 4 else 11 - place
            high, low = split(cur[part, plane])
            rows, columns = pl.ds(place * 32, 32), pl.ds(part * 512, 512)
            rhs[0, rows, columns] = high
            rhs[1, rows, columns] = low
    load_nt.wait()
    transform_and_send(t1, r1, send1, recv1)
    load_nn.wait()
    receive_all(t1, r1, send1, recv1)

    def gather1(q, carry):
        rows = pl.ds(pl.multiple_of((q // 4) * 32, 32), 32)
        first = lax.rem(q, 4) * 4
        pieces = [r1[0, first + i, rows, :] - r1[1, first + i, rows, :] for i in range(4)]
        columns = pl.ds(pl.multiple_of(q * 128, 128), 128)
        for p, piece in enumerate(regroup(pieces)):
            high, low = split(piece)
            lhs1[p * 32 : p * 32 + 32, columns] = high
            lhs1[128 + p * 32 : 160 + p * 32, columns] = low
        return carry

    lax.fori_loop(0, 8, gather1, 0)
    kernel_copy(0).wait_recv()
    kernel_copy(1).wait_recv()

    def product(n, carry):
        def spectrum(part):
            columns = pl.ds(pl.multiple_of(part * 512 + n * 256, 256), 256)
            both = dot_nn(lhs1[...], nn[0, :, columns])
            return both[:128] + both[128:] + dot_nn(lhs1[:128], nn[1, :, columns])

        re, im = spectrum(0), spectrum(1)
        ky = pl.ds(pl.multiple_of(n * 256, 256), 256)
        ky_im = pl.ds(pl.multiple_of(512 + n * 256, 256), 256)

        def multiply(kre, kim, rows):
            high, low = split(re * kim + im * kre)
            rhs[0, rows, ky] = high
            rhs[1, rows, ky] = low
            high, low = split(re * kre - im * kim)
            rhs[0, rows, ky_im] = high
            rhs[1, rows, ky_im] = low

        multiply(
            kern[0, 0:4, :, ky].reshape(128, 256),
            kern[1, 0:4, :, ky].reshape(128, 256),
            pl.ds(0, 128),
        )
        multiply(
            -jnp.concatenate([kmir[0, 3 - p, :, ky] for p in range(4)], axis=0),
            -jnp.concatenate([kmir[1, 3 - p, :, ky] for p in range(4)], axis=0),
            pl.ds(128, 128),
        )
        return carry

    lax.fori_loop(0, 2, product, 0)

    transform_and_send(t2, r2, send2, recv2)
    receive_all(t2, r2, send2, recv2)

    def gather2(q, carry):
        rows = pl.ds(pl.multiple_of((q // 4) * 32, 32), 32)
        first = lax.rem(q, 4) * 4
        columns = pl.ds(pl.multiple_of(q * 128, 128), 128)
        for side in range(2):
            pieces = [r2[side, first + i, rows, :] for i in range(4)]
            for p, piece in enumerate(regroup(pieces)):
                plane = 7 - p if side else p
                high, low = split(piece)
                lhs2[plane * 32 : plane * 32 + 32, columns] = high
                lhs2[256 + plane * 32 : 288 + plane * 32, columns] = low
        return carry

    lax.fori_loop(0, 8, gather2, 0)

    def finish(n, carry):
        columns = pl.ds(pl.multiple_of(n * 256, 256), 256)
        both = dot_nn(lhs2[...], nn[0, :, columns])
        value = both[:256] + both[256:] + dot_nn(lhs2[:256], nn[1, :, columns])
        x = pl.ds(pl.multiple_of(lax.rem(n, 2) * 256, 256), 256)
        out[1 - n // 2, :, :, x] = (value * scale).reshape(8, 32, 256)
        return carry

    lax.fori_loop(0, 4, finish, 0)
    kernel_copy(0).wait_send()
    kernel_copy(1).wait_send()
    sent_all(t1, r1, send1, recv1)
    sent_all(t2, r2, send2, recv2)


def local(current, kernel):
    members = lax.axis_size("gz")
    groups = lax.axis_size("gy")
    nt, nn = dft_tables(512, groups)
    vmem = pl.BlockSpec(memory_space=pltpu.VMEM)
    anywhere = pl.BlockSpec(memory_space=pl.ANY)
    exchange = pltpu.VMEM((2, groups, 64, 128), F32)
    return pl.pallas_call(
        functools.partial(body, members, groups, 1.0 / (512 * 512)),
        out_shape=jax.ShapeDtypeStruct(current.shape, F32),
        in_specs=[vmem, vmem, anywhere, anywhere],
        out_specs=vmem,
        scratch_shapes=[
            pltpu.VMEM((2, 1024, 1024), BF16),
            pltpu.VMEM((2, 1024, 1024), BF16),
            pltpu.VMEM((2, 256, 1024), BF16),
            pltpu.VMEM((256, 1024), BF16),
            pltpu.VMEM((512, 1024), BF16),
            pltpu.VMEM((2, 4, 32, 512), F32),
            exchange,
            exchange,
            exchange,
            exchange,
            pltpu.SemaphoreType.DMA((2,)),
            pltpu.SemaphoreType.DMA((2,)),
            pltpu.SemaphoreType.DMA((2,)),
            pltpu.SemaphoreType.DMA((32,)),
            pltpu.SemaphoreType.DMA((32,)),
            pltpu.SemaphoreType.DMA((32,)),
            pltpu.SemaphoreType.DMA((32,)),
        ],
        compiler_params=pltpu.CompilerParams(
            collective_id=0, has_side_effects=True, vmem_limit_bytes=48 * 1024 * 1024
        ),
    )(current, kernel, jnp.asarray(nt), jnp.asarray(nn))


def solution(mesh):
    spec = P(None, "gz", "gy", None)
    return jax.shard_map(
        local, mesh=mesh, in_specs=(spec, spec), out_specs=spec, check_vma=False
    )
```

profile of v0, /device:TPU:33, one launch (start us, length us, event | category | flops | bytes accessed | tf_op | source)
XLA Modules:
  0.0 154.4 jit_solution(13957254973053059027)
XLA Ops:
  0.0 0.0 copy-start
  0.0 1.2 copy-done
  1.2 0.0 copy-start.1
  1.2 1.2 copy-done.1
  2.5 150.9 %shard_map.46 = f32[2,8,32,512]{3,2,1,0:T(8,128)S(1)} custom-call(f32[2,8,32,512]{3,2,1,0:T(8,128)S(1)} %copy-done, f32[2,8,32,512]{3,2,1,0:T(8,128)S(1)} %copy-done.1, bf16[2,1024,1024]{2,1,0:T(8,128)(2,1)} %constant.4.clone.nt_hbm, bf16[2,1024,1024]{2,1,0:T(8,128)(2,1)} %constant.5.clone.nn_hbm), custom_call_target="tpu_custom_call" | custom-call | tf_op jit(solution)/shard_map/pallas_call | solution.py:284
  153.4 1.0 copy.6
Async XLA Ops:
  0.0 1.2 copy-start
  1.2 1.2 copy-start.1
where the time goes:
time: 155 us; the launch traced here: 154 us
  Pallas kernels  151 us (97%)
  local copies, waits for them, and re-layouts  3.42 us (2%)
    pallas_call x1, Pallas kernels, local(): pl.pallas_call(functools.partial(body, members, groups, 1.0 / (512 * 512)...  151 us
    unnamed x5, local copies, waits for them, and re-layouts  3.42 us

commit v1 on v0

v1 whole, which is shorter than its diff:
```python
import functools

import jax
import jax.numpy as jnp
import ml_dtypes
import numpy as np
from jax import lax
from jax.experimental import pallas as pl
from jax.experimental.pallas import tpu as pltpu
from jax.sharding import PartitionSpec as P

MESH = pl.DeviceIdType.MESH
F32 = jnp.float32
BF16 = jnp.bfloat16


def two_terms(table):
    high = table.astype(ml_dtypes.bfloat16)
    low = (table - high.astype(np.float64)).astype(ml_dtypes.bfloat16)
    return np.stack([high, low])


def dft_tables(length, groups):
    index = np.arange(length)
    angle = (index[:, None] * index[None, :] % length) * (2.0 * np.pi / length)
    cos, sin = np.cos(angle), np.sin(angle)
    full = np.block([[cos, sin], [-sin, cos]])
    block = length // groups
    rows = full.reshape(2, groups, block, 2 * length).transpose(1, 0, 2, 3)
    rows = rows.reshape(2 * length, 2 * length)
    return two_terms(rows), two_terms(full.T)


def split(value):
    high = value.astype(BF16)
    return high, (value - high.astype(F32)).astype(BF16)


def dot_nt(a, b):
    return lax.dot_general(a, b, (((1,), (1,)), ((), ())), preferred_element_type=F32)


def dot_nn(a, b):
    return jnp.dot(a, b, preferred_element_type=F32)


def regroup(pieces):
    lane = lax.broadcasted_iota(jnp.int32, pieces[0].shape, 1)
    low = lane < 64
    even = lax.rem(lane // 32, 2) == 0
    v0, v1, v2, v3 = pieces

    def halves(a, b):
        return (
            jnp.where(low, a, pltpu.roll(b, 64, 1)),
            jnp.where(low, pltpu.roll(a, 64, 1), b),
        )

    def quarters(a, b):
        return (
            jnp.where(even, a, pltpu.roll(b, 32, 1)),
            jnp.where(even, pltpu.roll(a, 96, 1), b),
        )

    a0, a2 = halves(v0, v2)
    a1, a3 = halves(v1, v3)
    return quarters(a0, a1) + quarters(a2, a3)


def body(
    members,
    scale,
    cur_hbm,
    kern_hbm,
    nt_hbm,
    nn_hbm,
    out,
    cur,
    kern,
    nt,
    nn,
    rhs,
    lhs,
    t1,
    met,
    diff,
    r1,
    t2,
    r2,
    load_sem,
    send1,
    recv1,
    send2,
    recv2,
    send3,
    recv3,
    send4,
    recv4,
):
    gz = lax.axis_index("gz")
    gy = lax.axis_index("gy")
    mirror = members - 1 - gz
    zh = gy // 4
    yc = lax.rem(gy, 4)
    side = gz // (members // 2)
    way = 1 - 2 * side
    sign = way.astype(F32)

    loads = [
        pltpu.make_async_copy(source, target, load_sem.at[i])
        for i, (source, target) in enumerate(
            [(cur_hbm, cur), (nt_hbm, nt), (nn_hbm, nn), (kern_hbm, kern)]
        )
    ]
    for load in loads:
        load.start()

    def column(dz):
        return lax.rem(zh + dz + 8, 4)

    def plane_at(place):
        return place + side * (7 - 2 * place)

    barrier = pltpu.get_barrier_semaphore()

    def greet(e, carry):
        other = column(lax.rem(e // 4, 4)) * 4 + lax.rem(yc + lax.rem(e, 4), 4)
        where = (gz + (e // 16) * (mirror - gz), other)
        pl.semaphore_signal(barrier, inc=1, device_id=where, device_id_type=MESH)
        return carry

    lax.fori_loop(1, 32, greet, 0)
    pl.semaphore_wait(barrier, 31)

    def rows_times_rhs(zb):
        rows = pl.ds(pl.multiple_of(zb * 256, 256), 256)
        high, low = nt[0, rows, :], nt[1, rows, :]
        return dot_nt(high, rhs[0]) + dot_nt(high, rhs[1]) + dot_nt(low, rhs[0])

    loads[0].wait()

    def take(place, carry):
        plane = plane_at(place)
        rows = pl.ds(pl.multiple_of(place * 32, 32), 32)
        for part in range(2):
            high, low = split(cur[part, plane])
            rhs[0, rows, part * 512 : part * 512 + 512] = high
            rhs[1, rows, part * 512 : part * 512 + 512] = low
        return carry

    lax.fori_loop(0, 8, take, 0)
    loads[1].wait()

    def forward_rows(dz):
        zb = column(dz)
        total = rows_times_rhs(zb)
        t1[0, pl.ds(zb * 4, 4)] = total[:, :128].reshape(4, 64, 128)
        t1[1, pl.ds(zb * 4, 4)] = total[:, 128:].reshape(4, 64, 128)

    def unit(k, by_side):
        along = way if by_side is side else -way
        return [(2, by_side), (along, 0), (along, 1), (0, by_side)][k]

    other_side = 1 - side

    def swap_copy(k):
        dz, half = unit(k, side)
        return pltpu.make_async_remote_copy(
            src_ref=t1.at[half, pl.ds(column(dz) * 4, 4)],
            dst_ref=met.at[k],
            send_sem=send1.at[k],
            recv_sem=recv1.at[k],
            device_id=(mirror, gy),
            device_id_type=MESH,
        )

    def subtract(k):
        dz, half = unit(k, other_side)
        diff[k] = (t1[half, pl.ds(column(dz) * 4, 4)] - met[k]) * sign

    def spread_copy(k, dy):
        dz, half = unit(k, other_side)
        yb = lax.rem(yc + dy, 4)
        target = gz if k == 3 else mirror
        return pltpu.make_async_remote_copy(
            src_ref=diff.at[k, yb],
            dst_ref=r1.at[half, gy],
            send_sem=send2.at[k * 4 + dy],
            recv_sem=recv2.at[k * 4 + dy],
            device_id=(target, column(dz) * 4 + yb),
            device_id_type=MESH,
        )

    def hand_copy(k):
        dz, half = unit(k, side)
        if k == 3:
            half = other_side
        rows = pl.ds(column(-dz) * 4, 4)
        return pltpu.make_async_remote_copy(
            src_ref=r1.at[half, rows],
            dst_ref=r1.at[half, rows],
            send_sem=send3.at[k],
            recv_sem=recv3.at[k],
            device_id=(mirror, gy),
            device_id_type=MESH,
        )

    def meet(k):
        swap_copy(k).wait_recv()
        subtract(k)

        def start(dy, carry):
            spread_copy(k, dy).start()
            return carry

        if k == 3:
            r1[other_side, gy] = diff[3, yc]
        lax.fori_loop(1 if k == 3 else 0, 4, start, 0)

    def hand(k):
        def wait(dy, carry):
            spread_copy(k, dy).wait_recv()
            return carry

        lax.fori_loop(1 if k == 3 else 0, 4, wait, 0)
        hand_copy(k).start()

    forward_rows(2)
    swap_copy(0).start()
    forward_rows(way)
    swap_copy(1).start()
    forward_rows(0)
    forward_rows(-way)
    swap_copy(2).start()
    meet(0)
    swap_copy(3).start()
    meet(1)
    hand(0)
    meet(2)
    hand(1)
    meet(3)
    hand(2)
    hand(3)
    loads[2].wait()
    loads[3].wait()
    for k in range(4):
        hand_copy(k).wait_recv()

    def gather(read, row_of):
        def one(q, carry):
            rows = pl.ds(pl.multiple_of((q // 4) * 32, 32), 32)
            first = lax.rem(q, 4) * 4
            columns = pl.ds(pl.multiple_of(q * 128, 128), 128)
            for half in range(2):
                pieces = [read(half, first + i, rows) for i in range(4)]
                for p, piece in enumerate(regroup(pieces)):
                    high, low = split(piece)
                    start = row_of(half * 4 + p) * 32
                    lhs[0, pl.ds(pl.multiple_of(start, 32), 32), columns] = high
                    lhs[1, pl.ds(pl.multiple_of(start, 32), 32), columns] = low
            return carry

        lax.fori_loop(0, 8, one, 0)

    def lhs_times(columns):
        both = dot_nn(lhs[...].reshape(512, 1024), nn[0, :, columns])
        return both[:256] + both[256:] + dot_nn(lhs[0], nn[1, :, columns])

    gather(lambda half, s, rows: r1[half, s, rows, :], lambda place: place)

    def product(n, carry):
        ky = pl.ds(pl.multiple_of(n * 256, 256), 256)
        ky_im = pl.ds(pl.multiple_of(512 + n * 256, 256), 256)
        re, im = lhs_times(ky), lhs_times(ky_im)
        kre = jnp.concatenate([kern[0, plane_at(p), :, ky] for p in range(8)], axis=0)
        kim = jnp.concatenate([kern[1, plane_at(p), :, ky] for p in range(8)], axis=0)
        high, low = split(re * kim + im * kre)
        rhs[0, :, ky] = high
        rhs[1, :, ky] = low
        high, low = split(re * kre - im * kim)
        rhs[0, :, ky_im] = high
        rhs[1, :, ky_im] = low
        return carry

    lax.fori_loop(0, 2, product, 0)

    def return_copy(e):
        other = column(e // 4) * 4 + lax.rem(yc + e, 4)
        return pltpu.make_async_remote_copy(
            src_ref=t2.at[other],
            dst_ref=r2.at[gy],
            send_sem=send4.at[e],
            recv_sem=recv4.at[e],
            device_id=(gz, other),
            device_id_type=MESH,
        )

    def inverse_rows(i, carry):
        dz = lax.rem(2 + 3 * i + 3 * (i * (i + 3) // 2 - 2 * i), 4)
        zb = column(dz)
        t2[pl.ds(zb * 4, 4)] = rows_times_rhs(zb).reshape(4, 64, 256)

        def start(dy, inner):
            e = dz * 4 + dy

            @pl.when(e > 0)
            def _():
                return_copy(e).start()

            return inner

        return lax.fori_loop(0, 4, start, carry)

    lax.fori_loop(0, 4, inverse_rows, 0)
    r2[gy] = t2[gy]

    def arrived(e, carry):
        return_copy(e).wait_recv()
        return carry

    lax.fori_loop(1, 16, arrived, 0)

    def read_back(half, s, rows):
        return r2[s, rows, half * 128 : half * 128 + 128]

    gather(read_back, plane_at)
    factor = sign * scale

    def finish(n, carry):
        columns = pl.ds(pl.multiple_of(n * 256, 256), 256)
        x = pl.ds(pl.multiple_of(lax.rem(n, 2) * 256, 256), 256)
        out[1 - n // 2, :, :, x] = (lhs_times(columns) * factor).reshape(8, 32, 256)
        return carry

    lax.fori_loop(0, 4, finish, 0)

    def sent(e, carry):
        return_copy(e).wait_send()
        return carry

    lax.fori_loop(1, 16, sent, 0)
    for k in range(4):
        swap_copy(k).wait_send()
        hand_copy(k).wait_send()
        for dy in range(1 if k == 3 else 0, 4):
            spread_copy(k, dy).wait_send()


def local(current, kernel):
    members = lax.axis_size("gz")
    groups = lax.axis_size("gy")
    nt, nn = dft_tables(512, groups)
    anywhere = pl.BlockSpec(memory_space=pl.ANY)
    table = pltpu.VMEM((2, 1024, 1024), BF16)
    operand = pltpu.VMEM((2, 256, 1024), BF16)
    block = pltpu.VMEM(current.shape, F32)
    halves = pltpu.VMEM((2, groups, 64, 128), F32)
    units = pltpu.VMEM((4, 4, 64, 128), F32)
    whole = pltpu.VMEM((groups, 64, 256), F32)
    dma = pltpu.SemaphoreType.DMA
    return pl.pallas_call(
        functools.partial(body, members, 1.0 / (512 * 512)),
        out_shape=jax.ShapeDtypeStruct(current.shape, F32),
        in_specs=[anywhere] * 4,
        out_specs=pl.BlockSpec(memory_space=pltpu.VMEM),
        scratch_shapes=[block, block, table, table, operand, operand]
        + [halves, units, units, halves, whole, whole]
        + [dma((4,)), dma((4,)), dma((4,)), dma((16,)), dma((16,))]
        + [dma((4,)), dma((4,)), dma((16,)), dma((16,))],
        compiler_params=pltpu.CompilerParams(
            collective_id=0, has_side_effects=True, vmem_limit_bytes=56 * 1024 * 1024
        ),
    )(current, kernel, jnp.asarray(nt), jnp.asarray(nn))


def solution(mesh):
    spec = P(None, "gz", "gy", None)
    return jax.shard_map(
        local, mesh=mesh, in_specs=(spec, spec), out_specs=spec, check_vma=False
    )
```

time: 155 us -> 140 us (0.903)
  the two profiles are of different devices: /device:TPU:33 before, /device:TPU:72 now
where the time goes in v1:
time: 140 us
  Pallas kernels  138 us (99%)
  local copies, waits for them, and re-layouts  2.29 us (2%)
    pallas_call x1, Pallas kernels, local(): pl.pallas_call(functools.partial(body, members, 1.0 / (512 * 512)), out_s...  138 us

profile of v1, /device:TPU:72, one launch (start us, length us, event | category | flops | bytes accessed | tf_op | source)
XLA Modules:
  0.0 140.1 jit_solution(10568111267071276205)
XLA Ops:
  0.0 137.8 %shard_map.46 = f32[2,8,32,512]{3,2,1,0:T(8,128)} custom-call(f32[2,8,32,512]{3,2,1,0:T(8,128)} %cur_hbm.1, f32[2,8,32,512]{3,2,1,0:T(8,128)} %kern_hbm.1, bf16[2,1024,1024]{2,1,0:T(8,128)(2,1)} %constant.4.clone.nt_hbm, bf16[2,1024,1024]{2,1,0:T(8,128)(2,1)} %constant.5.clone.nn_hbm), custom_call_target="tpu_custom_call" | custom-call | tf_op jit(solution)/shard_map/pallas_call | solution.py:361
  137.8 2.3 %copy.6 = f32[2,8,32,512]{3,2,1,0:T(8,128)} copy(f32[2,8,32,512]{3,2,1,0:T(8,128)} %shard_map.46) | data formatting | bytes 2097152

commit v2 on v1

--- a/solution.py
+++ b/solution.py
@@ -96,6 +96,9 @@
     recv3,
     send4,
     recv4,
+    relayed,
+    send5,
+    recv5,
 ):
     gz = lax.axis_index("gz")
     gy = lax.axis_index("gy")
@@ -130,7 +133,6 @@
         return carry
 
     lax.fori_loop(1, 32, greet, 0)
-    pl.semaphore_wait(barrier, 31)
 
     def rows_times_rhs(zb):
         rows = pl.ds(pl.multiple_of(zb * 256, 256), 256)
@@ -226,6 +228,7 @@
         hand_copy(k).start()
 
     forward_rows(2)
+    pl.semaphore_wait(barrier, 31)
     swap_copy(0).start()
     forward_rows(way)
     swap_copy(1).start()
@@ -295,6 +298,32 @@
             device_id_type=MESH,
         )
 
+    def up_or_down(dy):
+        return 1 - 2 * (dy // 2)
+
+    def first_leg(dy):
+        yb = lax.rem(yc + dy, 4)
+        return pltpu.make_async_remote_copy(
+            src_ref=t2.at[column(2) * 4 + yb],
+            dst_ref=relayed.at[dy],
+            send_sem=send5.at[dy],
+            recv_sem=recv5.at[dy],
+            device_id=(gz, column(up_or_down(dy)) * 4 + yb),
+            device_id_type=MESH,
+        )
+
+    def second_leg(dy):
+        step = up_or_down(dy)
+        origin = column(-step) * 4 + lax.rem(yc + 4 - dy, 4)
+        return pltpu.make_async_remote_copy(
+            src_ref=relayed.at[dy],
+            dst_ref=r2.at[origin],
+            send_sem=send4.at[8 + dy],
+            recv_sem=recv4.at[8 + dy],
+            device_id=(gz, column(step) * 4 + yc),
+            device_id_type=MESH,
+        )
+
     def inverse_rows(i, carry):
         dz = lax.rem(2 + 3 * i + 3 * (i * (i + 3) // 2 - 2 * i), 4)
         zb = column(dz)
@@ -303,10 +332,14 @@
         def start(dy, inner):
             e = dz * 4 + dy
 
-            @pl.when(e > 0)
+            @pl.when((e > 0) & (dz != 2))
             def _():
                 return_copy(e).start()
 
+            @pl.when(dz == 2)
+            def _():
+                first_leg(dy).start()
+
             return inner
 
         return lax.fori_loop(0, 4, start, carry)
@@ -314,11 +347,24 @@
     lax.fori_loop(0, 4, inverse_rows, 0)
     r2[gy] = t2[gy]
 
+    def relay(dy, carry):
+        first_leg(dy).wait_recv()
+        second_leg(dy).start()
+        return carry
+
+    lax.fori_loop(0, 4, relay, 0)
+
     def arrived(e, carry):
         return_copy(e).wait_recv()
         return carry
 
-    lax.fori_loop(1, 16, arrived, 0)
+    def arrived_relayed(dy, carry):
+        second_leg(dy).wait_recv()
+        return carry
+
+    lax.fori_loop(1, 8, arrived, 0)
+    lax.fori_loop(12, 16, arrived, 0)
+    lax.fori_loop(0, 4, arrived_relayed, 0)
 
     def read_back(half, s, rows):
         return r2[s, rows, half * 128 : half * 128 + 128]
@@ -338,7 +384,14 @@
         return_copy(e).wait_send()
         return carry
 
-    lax.fori_loop(1, 16, sent, 0)
+    def sent_relayed(dy, carry):
+        first_leg(dy).wait_send()
+        second_leg(dy).wait_send()
+        return carry
+
+    lax.fori_loop(1, 8, sent, 0)
+    lax.fori_loop(12, 16, sent, 0)
+    lax.fori_loop(0, 4, sent_relayed, 0)
     for k in range(4):
         swap_copy(k).wait_send()
         hand_copy(k).wait_send()
@@ -366,7 +419,8 @@
         scratch_shapes=[block, block, table, table, operand, operand]
         + [halves, units, units, halves, whole, whole]
         + [dma((4,)), dma((4,)), dma((4,)), dma((16,)), dma((16,))]
-        + [dma((4,)), dma((4,)), dma((16,)), dma((16,))],
+        + [dma((4,)), dma((4,)), dma((16,)), dma((16,))]
+        + [pltpu.VMEM((4, 64, 256), F32), dma((4,)), dma((4,))],
         compiler_params=pltpu.CompilerParams(
             collective_id=0, has_side_effects=True, vmem_limit_bytes=56 * 1024 * 1024
         ),

time: 140 us -> 138 us (0.986)
  the two profiles are of different devices: /device:TPU:72 before, /device:TPU:64 now
where the time goes in v2:
time: 138 us
  Pallas kernels  136 us (99%)
  local copies, waits for them, and re-layouts  2.29 us (2%)
    pallas_call x1, Pallas kernels, local(): pl.pallas_call(functools.partial(body, members, 1.0 / (512 * 512)), out_s...  136 us

profile of v2, /device:TPU:64, one launch (start us, length us, event | category | flops | bytes accessed | tf_op | source)
XLA Modules:
  0.0 138.0 jit_solution(9770542938059828205)
XLA Ops:
  0.0 135.7 %shard_map.46 = f32[2,8,32,512]{3,2,1,0:T(8,128)} custom-call(f32[2,8,32,512]{3,2,1,0:T(8,128)} %cur_hbm.1, f32[2,8,32,512]{3,2,1,0:T(8,128)} %kern_hbm.1, bf16[2,1024,1024]{2,1,0:T(8,128)(2,1)} %constant.4.clone.nt_hbm, bf16[2,1024,1024]{2,1,0:T(8,128)(2,1)} %constant.5.clone.nn_hbm), custom_call_target="tpu_custom_call" | custom-call | tf_op jit(solution)/shard_map/pallas_call | solution.py:414
  135.7 2.3 %copy.6 = f32[2,8,32,512]{3,2,1,0:T(8,128)} copy(f32[2,8,32,512]{3,2,1,0:T(8,128)} %shard_map.46) | data formatting | bytes 2097152

commit v3 on v1

v3 whole, which is shorter than its diff:
```python
import functools

import jax
import jax.numpy as jnp
import ml_dtypes
import numpy as np
from jax import lax
from jax.experimental import pallas as pl
from jax.experimental.pallas import tpu as pltpu
from jax.sharding import PartitionSpec as P

MESH = pl.DeviceIdType.MESH
F32 = jnp.float32
BF16 = jnp.bfloat16


def two_terms(table):
    high = table.astype(ml_dtypes.bfloat16)
    low = (table - high.astype(np.float64)).astype(ml_dtypes.bfloat16)
    return np.stack([high, low])


def dft_tables(length, groups):
    index = np.arange(length)
    angle = (index[:, None] * index[None, :] % length) * (2.0 * np.pi / length)
    cos, sin = np.cos(angle), np.sin(angle)
    full = np.block([[cos, sin], [-sin, cos]])
    half = length // groups // 2
    rows = full.reshape(2, groups, 2, half, 2 * length).transpose(1, 2, 0, 3, 4)
    rows = rows.reshape(2 * length, 2 * length)
    return two_terms(rows), two_terms(full.T)


def split(value):
    high = value.astype(BF16)
    return high, (value - high.astype(F32)).astype(BF16)


def dot_nt(a, b):
    return lax.dot_general(a, b, (((1,), (1,)), ((), ())), preferred_element_type=F32)


def dot_nn(a, b):
    return jnp.dot(a, b, preferred_element_type=F32)


def regroup(pieces):
    lane = lax.broadcasted_iota(jnp.int32, pieces[0].shape, 1)
    low = lane < 64
    even = lax.rem(lane // 32, 2) == 0
    v0, v1, v2, v3 = pieces

    def halves(a, b):
        return (
            jnp.where(low, a, pltpu.roll(b, 64, 1)),
            jnp.where(low, pltpu.roll(a, 64, 1), b),
        )

    def quarters(a, b):
        return (
            jnp.where(even, a, pltpu.roll(b, 32, 1)),
            jnp.where(even, pltpu.roll(a, 96, 1), b),
        )

    a0, a2 = halves(v0, v2)
    a1, a3 = halves(v1, v3)
    return quarters(a0, a1) + quarters(a2, a3)


def body(
    members,
    scale,
    cur_hbm,
    kern_hbm,
    nt_hbm,
    nn_hbm,
    out,
    cur,
    kern,
    nt,
    nn,
    rhs,
    back,
    lhs,
    t1,
    met,
    diff,
    r1,
    t2,
    r2,
    load_sem,
    send1,
    recv1,
    send2,
    recv2,
    send3,
    recv3,
    send4,
    recv4,
):
    gz = lax.axis_index("gz")
    gy = lax.axis_index("gy")
    mirror = members - 1 - gz
    zh = gy // 4
    yc = lax.rem(gy, 4)
    side = gz // (members // 2)
    other_side = 1 - side
    way = 1 - 2 * side
    sign = way.astype(F32)

    def column(dz):
        return lax.rem(zh + dz + 8, 4)

    def plane_at(place):
        return place + side * (7 - 2 * place)

    def table_rows(dz):
        return pl.ds(pl.multiple_of(column(dz) * 256, 256), 256)

    order = (2, way, 0, -way)
    load_cur = pltpu.make_async_copy(cur_hbm, cur, load_sem.at[0])
    load_kern = pltpu.make_async_copy(kern_hbm, kern, load_sem.at[1])
    load_nn = pltpu.make_async_copy(nn_hbm, nn, load_sem.at[2])
    load_nt = [
        pltpu.make_async_copy(
            nt_hbm.at[:, table_rows(dz)], nt.at[:, table_rows(dz)], load_sem.at[3 + i]
        )
        for i, dz in enumerate(order)
    ]
    load_cur.start()
    for load in load_nt:
        load.start()

    barrier = pltpu.get_barrier_semaphore()

    def greet(e, carry):
        other = column(lax.rem(e // 4, 4)) * 4 + lax.rem(yc + lax.rem(e, 4), 4)
        where = (gz + (e // 16) * (mirror - gz), other)
        pl.semaphore_signal(barrier, inc=1, device_id=where, device_id_type=MESH)
        return carry

    lax.fori_loop(1, 32, greet, 0)

    load_cur.wait()

    def take(place, carry):
        plane = plane_at(place)
        rows = pl.ds(pl.multiple_of(place * 32, 32), 32)
        for part in range(2):
            high, low = split(cur[part, plane])
            rhs[0, rows, part * 512 : part * 512 + 512] = high
            rhs[1, rows, part * 512 : part * 512 + 512] = low
        return carry

    lax.fori_loop(0, 8, take, 0)

    def forward_rows(i):
        load_nt[i].wait()
        high, low = nt[0, table_rows(order[i]), :], nt[1, table_rows(order[i]), :]
        total = dot_nt(high, rhs[0]) + dot_nt(high, rhs[1]) + dot_nt(low, rhs[0])
        targets = pl.ds(column(order[i]) * 4, 4)
        t1[0, targets] = total[:, :128].reshape(4, 64, 128)
        t1[1, targets] = total[:, 128:].reshape(4, 64, 128)

    slots = (pl.ds(64, 32), pl.ds(0, 64), pl.ds(96, 32))

    def half_rows(which):
        return pl.ds(pl.multiple_of(which * 32, 32), 32)

    def unit(u, which, along):
        rows = pl.ds(0, 64) if u == 1 else half_rows(which)
        return (2, along, 0)[u], rows

    def swap_copy(h, u):
        dz, rows = unit(u, side, way)
        return pltpu.make_async_remote_copy(
            src_ref=t1.at[h, pl.ds(column(dz) * 4, 4), rows],
            dst_ref=met.at[h, :, slots[u]],
            send_sem=send1.at[h * 3 + u],
            recv_sem=recv1.at[h * 3 + u],
            device_id=(mirror, gy),
            device_id_type=MESH,
        )

    def spread_copy(h, u, dy):
        dz, rows = unit(u, other_side, -way)
        yb = lax.rem(yc + dy, 4)
        target = gz if u == 2 else mirror
        return pltpu.make_async_remote_copy(
            src_ref=diff.at[h, yb, slots[u]],
            dst_ref=r1.at[h, gy, rows],
            send_sem=send2.at[h * 12 + u * 4 + dy],
            recv_sem=recv2.at[h * 12 + u * 4 + dy],
            device_id=(target, column(dz) * 4 + yb),
            device_id_type=MESH,
        )

    def hand_copy(h, u):
        dz, rows = unit(u, other_side if u == 2 else side, way)
        sources = pl.ds(column(-dz) * 4, 4)
        return pltpu.make_async_remote_copy(
            src_ref=r1.at[h, sources, rows],
            dst_ref=r1.at[h, sources, rows],
            send_sem=send3.at[h * 3 + u],
            recv_sem=recv3.at[h * 3 + u],
            device_id=(mirror, gy),
            device_id_type=MESH,
        )

    def meet(h, u):
        swap_copy(h, u).wait_recv()
        dz, rows = unit(u, other_side, -way)
        mine = t1[h, pl.ds(column(dz) * 4, 4), rows, :]
        diff[h, :, slots[u], :] = (mine - met[h, :, slots[u], :]) * sign

        def start(dy, carry):
            spread_copy(h, u, dy).start()
            return carry

        if u == 2:
            r1[h, gy, rows, :] = diff[h, yc, slots[u], :]
        lax.fori_loop(1 if u == 2 else 0, 4, start, 0)

    def hand(h, u):
        def wait(dy, carry):
            spread_copy(h, u, dy).wait_recv()
            return carry

        lax.fori_loop(1 if u == 2 else 0, 4, wait, 0)
        hand_copy(h, u).start()

    def gather(r, h, row_of):
        def one(q, carry):
            part = q // 4
            first = lax.rem(q, 4) * 4
            columns = pl.ds(pl.multiple_of(q * 128, 128), 128)
            upper = pl.ds(pl.multiple_of(part * 16, 16), 16)
            lower = pl.ds(pl.multiple_of(32 + part * 16, 16), 16)
            pieces = [
                jnp.concatenate([r[h, first + i, upper, :], r[h, first + i, lower, :]], axis=0)
                for i in range(4)
            ]
            for p, piece in enumerate(regroup(pieces)):
                high, low = split(piece)
                rows = pl.ds(pl.multiple_of(row_of(p) * 32, 32), 32)
                lhs[0, rows, columns] = high
                lhs[1, rows, columns] = low
            return carry

        lax.fori_loop(0, 8, one, 0)

    def lhs_times(columns):
        both = dot_nn(lhs[...].reshape(256, 1024), nn[0, :, columns])
        return both[:128] + both[128:] + dot_nn(lhs[0], nn[1, :, columns])

    def return_copy(h, e):
        other = column(e // 4) * 4 + lax.rem(yc + e, 4)
        return pltpu.make_async_remote_copy(
            src_ref=t2.at[h, other],
            dst_ref=r2.at[h, gy],
            send_sem=send4.at[h * 16 + e],
            recv_sem=recv4.at[h * 16 + e],
            device_id=(gz, other),
            device_id_type=MESH,
        )

    def middle(h):
        for u in range(3):
            hand_copy(h, u).wait_recv()

        gather(r1, h, lambda p: p)

        def product(n, carry):
            ky = pl.ds(pl.multiple_of(n * 256, 256), 256)
            ky_im = pl.ds(pl.multiple_of(512 + n * 256, 256), 256)
            re, im = lhs_times(ky), lhs_times(ky_im)
            planes = [plane_at(4 * h + p) for p in range(4)]
            kre = jnp.concatenate([kern[0, plane, :, ky] for plane in planes], axis=0)
            kim = jnp.concatenate([kern[1, plane, :, ky] for plane in planes], axis=0)
            high, low = split(re * kim + im * kre)
            back[0:128, ky] = high
            back[128:256, ky] = low
            high, low = split(re * kre - im * kim)
            back[0:128, ky_im] = high
            back[128:256, ky_im] = low
            return carry

        lax.fori_loop(0, 2, product, 0)

        def inverse_rows(i, carry):
            dz = lax.rem(2 + 3 * i + 3 * (i * (i + 3) // 2 - 2 * i), 4)
            both = dot_nt(nt[0, table_rows(dz), :], back[...])
            total = both[:, :128] + both[:, 128:]
            total += dot_nt(nt[1, table_rows(dz), :], back[0:128])
            t2[h, pl.ds(column(dz) * 4, 4)] = total.reshape(4, 64, 128)

            def start(dy, inner):
                e = dz * 4 + dy

                @pl.when(e > 0)
                def _():
                    return_copy(h, e).start()

                return inner

            return lax.fori_loop(0, 4, start, carry)

        lax.fori_loop(0, 4, inverse_rows, 0)
        r2[h, gy] = t2[h, gy]

    factor = sign * scale

    def finish(h):
        def arrived(e, carry):
            return_copy(h, e).wait_recv()
            return carry

        lax.fori_loop(1, 16, arrived, 0)
        gather(r2, h, lambda p: p)

        def columns_of(n, carry):
            columns = pl.ds(pl.multiple_of(n * 256, 256), 256)
            x = pl.ds(pl.multiple_of(lax.rem(n, 2) * 256, 256), 256)
            value = lhs_times(columns) * factor
            for p in range(4):
                out[1 - n // 2, plane_at(4 * h + p), :, x] = value[p * 32 : p * 32 + 32]
            return carry

        lax.fori_loop(0, 4, columns_of, 0)

    forward_rows(0)
    pl.semaphore_wait(barrier, 31)
    swap_copy(0, 0).start()
    load_nn.start()
    load_kern.start()
    forward_rows(1)
    swap_copy(0, 1).start()
    forward_rows(2)
    swap_copy(0, 2).start()
    forward_rows(3)
    meet(0, 0)
    swap_copy(1, 0).start()
    meet(0, 1)
    swap_copy(1, 1).start()
    hand(0, 0)
    meet(0, 2)
    swap_copy(1, 2).start()
    hand(0, 1)
    meet(1, 0)
    hand(0, 2)
    meet(1, 1)
    hand(1, 0)
    meet(1, 2)
    load_nn.wait()
    load_kern.wait()
    middle(0)
    hand(1, 1)
    hand(1, 2)
    middle(1)
    finish(0)
    finish(1)

    for h in range(2):
        for u in range(3):
            swap_copy(h, u).wait_send()
            hand_copy(h, u).wait_send()
            for dy in range(1 if u == 2 else 0, 4):
                spread_copy(h, u, dy).wait_send()

        def sent(e, carry):
            return_copy(h, e).wait_send()
            return carry

        lax.fori_loop(1, 16, sent, 0)


def local(current, kernel):
    members = lax.axis_size("gz")
    groups = lax.axis_size("gy")
    nt, nn = dft_tables(512, groups)
    anywhere = pl.BlockSpec(memory_space=pl.ANY)
    table = pltpu.VMEM((2, 1024, 1024), BF16)
    block = pltpu.VMEM(current.shape, F32)
    halves = pltpu.VMEM((2, groups, 64, 128), F32)
    units = pltpu.VMEM((2, 4, 128, 128), F32)
    dma = pltpu.SemaphoreType.DMA
    return pl.pallas_call(
        functools.partial(body, members, 1.0 / (512 * 512)),
        out_shape=jax.ShapeDtypeStruct(current.shape, F32),
        in_specs=[anywhere] * 4,
        out_specs=pl.BlockSpec(memory_space=pltpu.VMEM),
        scratch_shapes=[block, block, table, table]
        + [pltpu.VMEM((2, 256, 1024), BF16), pltpu.VMEM((256, 1024), BF16)]
        + [pltpu.VMEM((2, 128, 1024), BF16)]
        + [halves, units, units, halves, halves, halves]
        + [dma((7,)), dma((6,)), dma((6,)), dma((24,)), dma((24,))]
        + [dma((6,)), dma((6,)), dma((32,)), dma((32,))],
        compiler_params=pltpu.CompilerParams(
            collective_id=0, has_side_effects=True, vmem_limit_bytes=48 * 1024 * 1024
        ),
    )(current, kernel, jnp.asarray(nt), jnp.asarray(nn))


def solution(mesh):
    spec = P(None, "gz", "gy", None)
    return jax.shard_map(
        local, mesh=mesh, in_specs=(spec, spec), out_specs=spec, check_vma=False
    )
```

time: 140 us -> 136 us (0.971)
  the two profiles are of different devices: /device:TPU:72 before, /device:TPU:32 now
where the time goes in v3:
time: 136 us
  Pallas kernels  132 us (97%)
  local copies, waits for them, and re-layouts  3.42 us (3%)
    pallas_call x1, Pallas kernels, local(): pl.pallas_call(functools.partial(body, members, 1.0 / (512 * 512)), out_s...  132 us
    unnamed x5, local copies, waits for them, and re-layouts  3.42 us

profile of v3, /device:TPU:32, one launch (start us, length us, event | category | flops | bytes accessed | tf_op | source)
XLA Modules:
  0.0 135.8 jit_solution(14747002385254233147)
XLA Ops:
  0.0 0.0 copy-start
  0.0 1.2 copy-done
  1.2 0.0 copy-start.1
  1.2 1.2 copy-done.1
  2.5 132.3 %shard_map.46 = f32[2,8,32,512]{3,2,1,0:T(8,128)S(1)} custom-call(f32[2,8,32,512]{3,2,1,0:T(8,128)S(1)} %copy-done, f32[2,8,32,512]{3,2,1,0:T(8,128)S(1)} %copy-done.1, bf16[2,1024,1024]{2,1,0:T(8,128)(2,1)} %constant.4.clone.nt_hbm, bf16[2,1024,1024]{2,1,0:T(8,128)(2,1)} %constant.5.clone.nn_hbm), custom_call_target="tpu_custom_call" | custom-call | tf_op jit(solution)/shard_map/pallas_call | solution.py:387
  134.8 1.0 copy.6
Async XLA Ops:
  0.0 1.2 copy-start
  1.2 1.2 copy-start.1

commit v4 on v2

--- a/solution.py
+++ b/solution.py
@@ -28,7 +28,8 @@
     block = length // groups
     rows = full.reshape(2, groups, block, 2 * length).transpose(1, 0, 2, 3)
     rows = rows.reshape(2 * length, 2 * length)
-    return two_terms(rows), two_terms(full.T)
+    down = full.T.reshape(2, 4, length // 4, 2 * length).transpose(1, 0, 2, 3)
+    return two_terms(rows), two_terms(down.reshape(2 * length, 2 * length))
 
 
 def split(value):
@@ -81,6 +82,7 @@
     nn,
     rhs,
     lhs,
+    spectrum,
     t1,
     met,
     diff,
@@ -109,20 +111,28 @@
     way = 1 - 2 * side
     sign = way.astype(F32)
 
-    loads = [
-        pltpu.make_async_copy(source, target, load_sem.at[i])
-        for i, (source, target) in enumerate(
-            [(cur_hbm, cur), (nt_hbm, nt), (nn_hbm, nn), (kern_hbm, kern)]
-        )
-    ]
-    for load in loads:
-        load.start()
-
     def column(dz):
         return lax.rem(zh + dz + 8, 4)
 
     def plane_at(place):
         return place + side * (7 - 2 * place)
+
+    def table_rows(dz):
+        return pl.ds(pl.multiple_of(column(dz) * 256, 256), 256)
+
+    order = (2, way, 0, -way)
+    load_cur = pltpu.make_async_copy(cur_hbm, cur, load_sem.at[0])
+    load_kern = pltpu.make_async_copy(kern_hbm, kern, load_sem.at[1])
+    load_nn = pltpu.make_async_copy(nn_hbm, nn, load_sem.at[2])
+    load_nt = [
+        pltpu.make_async_copy(
+            nt_hbm.at[:, table_rows(dz)], nt.at[:, table_rows(dz)], load_sem.at[3 + i]
+        )
+        for i, dz in enumerate(order)
+    ]
+    load_cur.start()
+    for load in load_nt:
+        load.start()
 
     barrier = pltpu.get_barrier_semaphore()
 
@@ -134,12 +144,12 @@
 
     lax.fori_loop(1, 32, greet, 0)
 
-    def rows_times_rhs(zb):
-        rows = pl.ds(pl.multiple_of(zb * 256, 256), 256)
+    def rows_times_rhs(dz):
+        rows = table_rows(dz)
         high, low = nt[0, rows, :], nt[1, rows, :]
         return dot_nt(high, rhs[0]) + dot_nt(high, rhs[1]) + dot_nt(low, rhs[0])
 
-    loads[0].wait()
+    load_cur.wait()
 
     def take(place, carry):
         plane = plane_at(place)
@@ -151,11 +161,11 @@
         return carry
 
     lax.fori_loop(0, 8, take, 0)
-    loads[1].wait()
-
-    def forward_rows(dz):
-        zb = column(dz)
-        total = rows_times_rhs(zb)
+
+    def forward_rows(i):
+        load_nt[i].wait()
+        total = rows_times_rhs(order[i])
+        zb = column(order[i])
         t1[0, pl.ds(zb * 4, 4)] = total[:, :128].reshape(4, 64, 128)
         t1[1, pl.ds(zb * 4, 4)] = total[:, 128:].reshape(4, 64, 128)
 
@@ -227,13 +237,42 @@
         lax.fori_loop(1 if k == 3 else 0, 4, wait, 0)
         hand_copy(k).start()
 
-    forward_rows(2)
+    def gather(read, zb, row_of):
+        for part in range(2):
+            rows = pl.ds(part * 32, 32)
+            for half in range(2):
+                pieces = [read(half, zb * 4 + i, rows) for i in range(4)]
+                for p, piece in enumerate(regroup(pieces)):
+                    high, low = split(piece)
+                    start = pl.ds(pl.multiple_of(row_of(half * 4 + p) * 32, 32), 32)
+                    lhs[0, start, part * 128 : part * 128 + 128] = high
+                    lhs[1, start, part * 128 : part * 128 + 128] = low
+
+    def lhs_times(dz, columns):
+        rows = table_rows(dz)
+        both = dot_nn(lhs[...].reshape(512, 256), nn[0, rows, columns])
+        return both[:256] + both[256:] + dot_nn(lhs[0], nn[1, rows, columns])
+
+    def forward_from(dz, first):
+        gather(lambda half, s, rows: r1[half, s, rows, :], column(dz), lambda place: place)
+
+        def one(n, carry):
+            columns = pl.ds(pl.multiple_of(n * 256, 256), 256)
+            value = lhs_times(dz, columns)
+            spectrum[:, columns] = value if first else spectrum[:, columns] + value
+            return carry
+
+        lax.fori_loop(0, 4, one, 0)
+
+    forward_rows(0)
     pl.semaphore_wait(barrier, 31)
     swap_copy(0).start()
-    forward_rows(way)
+    load_nn.start()
+    load_kern.start()
+    forward_rows(1)
     swap_copy(1).start()
-    forward_rows(0)
-    forward_rows(-way)
+    forward_rows(2)
+    forward_rows(3)
     swap_copy(2).start()
     meet(0)
     swap_copy(3).start()
@@ -244,37 +283,21 @@
     meet(3)
     hand(2)
     hand(3)
-    loads[2].wait()
-    loads[3].wait()
-    for k in range(4):
-        hand_copy(k).wait_recv()
-
-    def gather(read, row_of):
-        def one(q, carry):
-            rows = pl.ds(pl.multiple_of((q // 4) * 32, 32), 32)
-            first = lax.rem(q, 4) * 4
-            columns = pl.ds(pl.multiple_of(q * 128, 128), 128)
-            for half in range(2):
-                pieces = [read(half, first + i, rows) for i in range(4)]
-                for p, piece in enumerate(regroup(pieces)):
-                    high, low = split(piece)
-                    start = row_of(half * 4 + p) * 32
-                    lhs[0, pl.ds(pl.multiple_of(start, 32), 32), columns] = high
-                    lhs[1, pl.ds(pl.multiple_of(start, 32), 32), columns] = low
-            return carry
-
-        lax.fori_loop(0, 8, one, 0)
-
-    def lhs_times(columns):
-        both = dot_nn(lhs[...].reshape(512, 1024), nn[0, :, columns])
-        return both[:256] + both[256:] + dot_nn(lhs[0], nn[1, :, columns])
-
-    gather(lambda half, s, rows: r1[half, s, rows, :], lambda place: place)
+    load_nn.wait()
+    forward_from(-way, True)
+    hand_copy(0).wait_recv()
+    forward_from(2, False)
+    hand_copy(1).wait_recv()
+    hand_copy(2).wait_recv()
+    forward_from(way, False)
+    hand_copy(3).wait_recv()
+    forward_from(0, False)
+    load_kern.wait()
 
     def product(n, carry):
         ky = pl.ds(pl.multiple_of(n * 256, 256), 256)
         ky_im = pl.ds(pl.multiple_of(512 + n * 256, 256), 256)
-        re, im = lhs_times(ky), lhs_times(ky_im)
+        re, im = spectrum[:, ky], spectrum[:, ky_im]
         kre = jnp.concatenate([kern[0, plane_at(p), :, ky] for p in range(8)], axis=0)
         kim = jnp.concatenate([kern[1, plane_at(p), :, ky] for p in range(8)], axis=0)
         high, low = split(re * kim + im * kre)
@@ -327,7 +350,7 @@
     def inverse_rows(i, carry):
         dz = lax.rem(2 + 3 * i + 3 * (i * (i + 3) // 2 - 2 * i), 4)
         zb = column(dz)
-        t2[pl.ds(zb * 4, 4)] = rows_times_rhs(zb).reshape(4, 64, 256)
+        t2[pl.ds(zb * 4, 4)] = rows_times_rhs(dz).reshape(4, 64, 256)
 
         def start(dy, inner):
             e = dz * 4 + dy
@@ -362,23 +385,32 @@
         second_leg(dy).wait_recv()
         return carry
 
-    lax.fori_loop(1, 8, arrived, 0)
+    factor = sign * scale
+
+    def back_from(dz, first):
+        def read(half, s, rows):
+            return r2[s, rows, half * 128 : half * 128 + 128]
+
+        gather(read, column(dz), plane_at)
+
+        def one(n, carry):
+            columns = pl.ds(pl.multiple_of(n * 256, 256), 256)
+            x = pl.ds(pl.multiple_of(lax.rem(n, 2) * 256, 256), 256)
+            value = (lhs_times(dz, columns) * factor).reshape(8, 32, 256)
+            part = 1 - n // 2
+            out[part, :, :, x] = value if first else out[part, :, :, x] + value
+            return carry
+
+        lax.fori_loop(0, 4, one, 0)
+
+    lax.fori_loop(1, 4, arrived, 0)
+    back_from(0, True)
+    lax.fori_loop(4, 8, arrived, 0)
+    back_from(-1, False)
     lax.fori_loop(12, 16, arrived, 0)
+    back_from(1, False)
     lax.fori_loop(0, 4, arrived_relayed, 0)
-
-    def read_back(half, s, rows):
-        return r2[s, rows, half * 128 : half * 128 + 128]
-
-    gather(read_back, plane_at)
-    factor = sign * scale
-
-    def finish(n, carry):
-        columns = pl.ds(pl.multiple_of(n * 256, 256), 256)
-        x = pl.ds(pl.multiple_of(lax.rem(n, 2) * 256, 256), 256)
-        out[1 - n // 2, :, :, x] = (lhs_times(columns) * factor).reshape(8, 32, 256)
-        return carry
-
-    lax.fori_loop(0, 4, finish, 0)
+    back_from(2, False)
 
     def sent(e, carry):
         return_copy(e).wait_send()
@@ -403,9 +435,13 @@
     members = lax.axis_size("gz")
     groups = lax.axis_size("gy")
     nt, nn = dft_tables(512, groups)
-    anywhere = pl.BlockSpec(memory_space=pl.ANY)
+    hbm = pl.BlockSpec(memory_space=pltpu.HBM)
     table = pltpu.VMEM((2, 1024, 1024), BF16)
-    operand = pltpu.VMEM((2, 256, 1024), BF16)
+    operands = [
+        pltpu.VMEM((2, 256, 1024), BF16),
+        pltpu.VMEM((2, 256, 256), BF16),
+        pltpu.VMEM((256, 1024), F32),
+    ]
     block = pltpu.VMEM(current.shape, F32)
     halves = pltpu.VMEM((2, groups, 64, 128), F32)
     units = pltpu.VMEM((4, 4, 64, 128), F32)
@@ -414,15 +450,16 @@
     return pl.pallas_call(
         functools.partial(body, members, 1.0 / (512 * 512)),
         out_shape=jax.ShapeDtypeStruct(current.shape, F32),
-        in_specs=[anywhere] * 4,
+        in_specs=[hbm] * 4,
         out_specs=pl.BlockSpec(memory_space=pltpu.VMEM),
-        scratch_shapes=[block, block, table, table, operand, operand]
+        scratch_shapes=[block, block, table, table]
+        + operands
         + [halves, units, units, halves, whole, whole]
-        + [dma((4,)), dma((4,)), dma((4,)), dma((16,)), dma((16,))]
+        + [dma((7,)), dma((4,)), dma((4,)), dma((16,)), dma((16,))]
         + [dma((4,)), dma((4,)), dma((16,)), dma((16,))]
         + [pltpu.VMEM((4, 64, 256), F32), dma((4,)), dma((4,))],
         compiler_params=pltpu.CompilerParams(
-            collective_id=0, has_side_effects=True, vmem_limit_bytes=56 * 1024 * 1024
+            collective_id=0, has_side_effects=True, vmem_limit_bytes=52 * 1024 * 1024
         ),
     )(current, kernel, jnp.asarray(nt), jnp.asarray(nn))
 

time: 138 us -> 131 us (0.949)
  Pallas kernels: 136 us -> 129 us
    pallas_call x1, Pallas kernels: 136 us -> 129 us  [local(): pl.pallas_call(functools.partial(body, members, 1.0 / (512 * 512)), out_s...]
where the time goes in v4:
time: 131 us; the launch traced here: 130 us
  Pallas kernels  129 us (98%)
    pallas_call x1, Pallas kernels, local(): pl.pallas_call(functools.partial(body, members, 1.0 / (512 * 512)), out_s...  129 us

profile of v4, /device:TPU:64, one launch (start us, length us, event | category | flops | bytes accessed | tf_op | source)
XLA Modules:
  0.0 130.3 jit_solution(12338657071846768467)
XLA Ops:
  0.0 129.3 %shard_map.46 = f32[2,8,32,512]{3,2,1,0:T(8,128)S(1)} custom-call(f32[2,8,32,512]{3,2,1,0:T(8,128)} %cur_hbm.1, f32[2,8,32,512]{3,2,1,0:T(8,128)} %kern_hbm.1, bf16[2,1024,1024]{2,1,0:T(8,128)(2,1)} %constant.4.clone.nt_hbm, bf16[2,1024,1024]{2,1,0:T(8,128)(2,1)} %constant.5.clone.nn_hbm), custom_call_target="tpu_custom_call" | custom-call | tf_op jit(solution)/shard_map/pallas_call | solution.py:450
  129.3 1.0 copy.6

commit v5 on v4

--- a/solution.py
+++ b/solution.py
@@ -322,7 +322,7 @@
         )
 
     def up_or_down(dy):
-        return 1 - 2 * (dy // 2)
+        return 1 - 2 * lax.rem(dy, 2)
 
     def first_leg(dy):
         yb = lax.rem(yc + dy, 4)
@@ -347,27 +347,29 @@
             device_id_type=MESH,
         )
 
-    def inverse_rows(i, carry):
-        dz = lax.rem(2 + 3 * i + 3 * (i * (i + 3) // 2 - 2 * i), 4)
-        zb = column(dz)
-        t2[pl.ds(zb * 4, 4)] = rows_times_rhs(dz).reshape(4, 64, 256)
-
-        def start(dy, inner):
-            e = dz * 4 + dy
-
-            @pl.when((e > 0) & (dz != 2))
-            def _():
-                return_copy(e).start()
-
-            @pl.when(dz == 2)
-            def _():
-                first_leg(dy).start()
-
-            return inner
-
-        return lax.fori_loop(0, 4, start, carry)
-
-    lax.fori_loop(0, 4, inverse_rows, 0)
+    def inverse_rows(dz):
+        t2[pl.ds(column(dz) * 4, 4)] = rows_times_rhs(dz).reshape(4, 64, 256)
+
+    def start_far(dy, carry):
+        first_leg(dy).start()
+        return carry
+
+    def start_near(dy, carry):
+        return_copy(4 + dy).start()
+        return_copy(12 + dy).start()
+        return carry
+
+    def start_own(dy, carry):
+        return_copy(dy).start()
+        return carry
+
+    inverse_rows(2)
+    lax.fori_loop(0, 4, start_far, 0)
+    inverse_rows(1)
+    inverse_rows(-1)
+    lax.fori_loop(0, 4, start_near, 0)
+    inverse_rows(0)
+    lax.fori_loop(1, 4, start_own, 0)
     r2[gy] = t2[gy]
 
     def relay(dy, carry):

time: 131 us -> 129 us (0.985)
  the two profiles are of different devices: /device:TPU:64 before, /device:TPU:72 now
where the time goes in v5:
time: 129 us
  Pallas kernels  128 us (99%)
    pallas_call x1, Pallas kernels, local(): pl.pallas_call(functools.partial(body, members, 1.0 / (512 * 512)), out_s...  128 us

profile of v5, /device:TPU:72, one launch (start us, length us, event | category | flops | bytes accessed | tf_op | source)
XLA Modules:
  0.0 129.1 jit_solution(6020271780210179059)
XLA Ops:
  0.0 128.1 %shard_map.46 = f32[2,8,32,512]{3,2,1,0:T(8,128)S(1)} custom-call(f32[2,8,32,512]{3,2,1,0:T(8,128)} %cur_hbm.1, f32[2,8,32,512]{3,2,1,0:T(8,128)} %kern_hbm.1, bf16[2,1024,1024]{2,1,0:T(8,128)(2,1)} %constant.4.clone.nt_hbm, bf16[2,1024,1024]{2,1,0:T(8,128)(2,1)} %constant.5.clone.nn_hbm), custom_call_target="tpu_custom_call" | custom-call | tf_op jit(solution)/shard_map/pallas_call | solution.py:452
  128.1 1.0 copy.6

commit v6 on v5

--- a/solution.py
+++ b/solution.py
@@ -173,6 +173,8 @@
         along = way if by_side is side else -way
         return [(2, by_side), (along, 0), (along, 1), (0, by_side)][k]
 
+    inner = lax.rem((gz * 4 // members + 1) // 2, 2)
+
     other_side = 1 - side
 
     def swap_copy(k):
@@ -357,6 +359,12 @@
     def start_near(dy, carry):
         return_copy(4 + dy).start()
         return_copy(12 + dy).start()
+
+        @pl.when(inner == 0)
+        def _():
+            return_copy(4 + dy).wait_send()
+            return_copy(12 + dy).wait_send()
+
         return carry
 
     def start_own(dy, carry):
@@ -423,8 +431,13 @@
         second_leg(dy).wait_send()
         return carry
 
-    lax.fori_loop(1, 8, sent, 0)
-    lax.fori_loop(12, 16, sent, 0)
+    lax.fori_loop(1, 4, sent, 0)
+
+    @pl.when(inner == 1)
+    def _():
+        lax.fori_loop(4, 8, sent, 0)
+        lax.fori_loop(12, 16, sent, 0)
+
     lax.fori_loop(0, 4, sent_relayed, 0)
     for k in range(4):
         swap_copy(k).wait_send()

time: 129 us -> 129 us (level)
  the two profiles are of different devices: /device:TPU:72 before, /device:TPU:71 now
where the time goes in v6:
time: 129 us
  Pallas kernels  128 us (99%)
    pallas_call x1, Pallas kernels, local(): pl.pallas_call(functools.partial(body, members, 1.0 / (512 * 512)), out_s...  128 us

profile of v6, /device:TPU:71, one launch (start us, length us, event | category | flops | bytes accessed | tf_op | source)
XLA Modules:
  0.0 128.9 jit_solution(3589128658906820827)
XLA Ops:
  0.0 128.0 %shard_map.46 = f32[2,8,32,512]{3,2,1,0:T(8,128)S(1)} custom-call(f32[2,8,32,512]{3,2,1,0:T(8,128)} %cur_hbm.1, f32[2,8,32,512]{3,2,1,0:T(8,128)} %kern_hbm.1, bf16[2,1024,1024]{2,1,0:T(8,128)(2,1)} %constant.4.clone.nt_hbm, bf16[2,1024,1024]{2,1,0:T(8,128)(2,1)} %constant.5.clone.nn_hbm), custom_call_target="tpu_custom_call" | custom-call | tf_op jit(solution)/shard_map/pallas_call | solution.py:465
  128.0 1.0 copy.6

commit v7 on v5

--- a/solution.py
+++ b/solution.py
@@ -98,9 +98,6 @@
     recv3,
     send4,
     recv4,
-    relayed,
-    send5,
-    recv5,
 ):
     gz = lax.axis_index("gz")
     gy = lax.axis_index("gy")
@@ -321,37 +318,11 @@
             device_id_type=MESH,
         )
 
-    def up_or_down(dy):
-        return 1 - 2 * lax.rem(dy, 2)
-
-    def first_leg(dy):
-        yb = lax.rem(yc + dy, 4)
-        return pltpu.make_async_remote_copy(
-            src_ref=t2.at[column(2) * 4 + yb],
-            dst_ref=relayed.at[dy],
-            send_sem=send5.at[dy],
-            recv_sem=recv5.at[dy],
-            device_id=(gz, column(up_or_down(dy)) * 4 + yb),
-            device_id_type=MESH,
-        )
-
-    def second_leg(dy):
-        step = up_or_down(dy)
-        origin = column(-step) * 4 + lax.rem(yc + 4 - dy, 4)
-        return pltpu.make_async_remote_copy(
-            src_ref=relayed.at[dy],
-            dst_ref=r2.at[origin],
-            send_sem=send4.at[8 + dy],
-            recv_sem=recv4.at[8 + dy],
-            device_id=(gz, column(step) * 4 + yc),
-            device_id_type=MESH,
-        )
-
     def inverse_rows(dz):
         t2[pl.ds(column(dz) * 4, 4)] = rows_times_rhs(dz).reshape(4, 64, 256)
 
     def start_far(dy, carry):
-        first_leg(dy).start()
+        return_copy(8 + dy).start()
         return carry
 
     def start_near(dy, carry):
@@ -372,19 +343,8 @@
     lax.fori_loop(1, 4, start_own, 0)
     r2[gy] = t2[gy]
 
-    def relay(dy, carry):
-        first_leg(dy).wait_recv()
-        second_leg(dy).start()
-        return carry
-
-    lax.fori_loop(0, 4, relay, 0)
-
     def arrived(e, carry):
         return_copy(e).wait_recv()
-        return carry
-
-    def arrived_relayed(dy, carry):
-        second_leg(dy).wait_recv()
         return carry
 
     factor = sign * scale
@@ -411,21 +371,14 @@
     back_from(-1, False)
     lax.fori_loop(12, 16, arrived, 0)
     back_from(1, False)
-    lax.fori_loop(0, 4, arrived_relayed, 0)
+    lax.fori_loop(8, 12, arrived, 0)
     back_from(2, False)
 
     def sent(e, carry):
         return_copy(e).wait_send()
         return carry
 
-    def sent_relayed(dy, carry):
-        first_leg(dy).wait_send()
-        second_leg(dy).wait_send()
-        return carry
-
-    lax.fori_loop(1, 8, sent, 0)
-    lax.fori_loop(12, 16, sent, 0)
-    lax.fori_loop(0, 4, sent_relayed, 0)
+    lax.fori_loop(1, 16, sent, 0)
     for k in range(4):
         swap_copy(k).wait_send()
         hand_copy(k).wait_send()
@@ -459,7 +412,7 @@
         + [halves, units, units, halves, whole, whole]
         + [dma((7,)), dma((4,)), dma((4,)), dma((16,)), dma((16,))]
         + [dma((4,)), dma((4,)), dma((16,)), dma((16,))]
-        + [pltpu.VMEM((4, 64, 256), F32), dma((4,)), dma((4,))],
+        + [],
         compiler_params=pltpu.CompilerParams(
             collective_id=0, has_side_effects=True, vmem_limit_bytes=52 * 1024 * 1024
         ),

time: 129 us -> 132 us (1.023)
  the two profiles are of different devices: /device:TPU:72 before, /device:TPU:64 now
where the time goes in v7:
time: 132 us
  Pallas kernels  131 us (99%)
    pallas_call x1, Pallas kernels, local(): pl.pallas_call(functools.partial(body, members, 1.0 / (512 * 512)), out_s...  131 us

profile of v7, /device:TPU:64, one launch (start us, length us, event | category | flops | bytes accessed | tf_op | source)
XLA Modules:
  0.0 132.2 jit_solution(1335645480150820948)
XLA Ops:
  0.0 131.2 %shard_map.46 = f32[2,8,32,512]{3,2,1,0:T(8,128)S(1)} custom-call(f32[2,8,32,512]{3,2,1,0:T(8,128)} %cur_hbm.1, f32[2,8,32,512]{3,2,1,0:T(8,128)} %kern_hbm.1, bf16[2,1024,1024]{2,1,0:T(8,128)(2,1)} %constant.4.clone.nt_hbm, bf16[2,1024,1024]{2,1,0:T(8,128)(2,1)} %constant.5.clone.nn_hbm), custom_call_target="tpu_custom_call" | custom-call | tf_op jit(solution)/shard_map/pallas_call | solution.py:405
  131.2 1.0 copy.6
